TPU v7x, 512 devices: a whole 4x4x16 slice. The times are simulated.
512 devices in a mesh: rows: 8 (over x_lo, y), cols: 64 (over z, x_hi, core).
Axes of the slice: x: 4 (x_hi: 2, x_lo: 2; x = x_hi * 2 + x_lo), y: 4, z: 16, core: 2. Of those that a mesh axis runs over, the one named last changes fastest.
Arguments:
- fronts: bfloat16 [8, 128, 16, 8192], P('rows', None, None, 'cols')
- factors: bfloat16 [8, 2048, 8192], P('rows', None, 'cols'), may hold values from -0.125 to 0.125
- site_tensors: float32 [8, 16, 4096], P('rows', None, 'cols'), may hold values from -6 to 6
- operators: float32 [8, 4, 256], P('rows', None, 'cols'), may hold values from -6 to 6
- kept_ranks: int32 [8, 64], P('rows', 'cols'), may hold values from 64 to 128, as said below
Outputs:
- next_fronts: bfloat16 [8, 128, 16, 8192], P('rows', None, None, 'cols')
Inputs may be any that keep to these rules, and one draw needn't show every extreme that they name: `kept_ranks`: each bond's kept rank is a multiple of 8; in every draw some bond keeps all 128.
All inputs are finite; a program needn't handle non-finite values. Where the computation divides by a largest or mean magnitude, that divisor is 1e-20 or more.
Results may differ from a plain program's by a relative error of at most 0.03.
Values may be sent and summed in bfloat16 or wider, within the bound.
A program may use at most 64 MiB of HBM per device.

v0:
```python
import jax
import jax.numpy as jnp
from jax import lax
from jax.sharding import PartitionSpec as P

X = 128
D = 4
S = 4


epsilon = 1e-06
block_rows = 16


def from_behind(block, axis, distance):
    devices = range(lax.axis_size(axis))
    route = [((i - distance) % len(devices), i) for i in devices]
    return lax.ppermute(block, axis, route)


def partner(value, axis, distance):
    mask = 2**distance
    pairs = [(source, source ^ mask) for source in range(lax.axis_size(axis))]
    return lax.ppermute(value, axis, pairs)


def double_layer(tensor, operator):
    return jnp.einsum("vlwqs,st,VLWQt->lLvVwWqQ", tensor, operator, tensor)


def per_device(fronts, factors, site_tensors, operators, kept_ranks):
    double_width = D * D
    tensor = site_tensors[0].reshape(D, D, D, D, S)
    operator = operators[0]
    downward = double_layer(tensor, operator)
    upward = double_layer(jnp.transpose(tensor, (2, 1, 0, 3, 4)), operator)
    odd_group = lax.axis_index("rows") % 2 == 1
    doubled = jnp.where(odd_group, upward, downward)
    doubled = doubled.reshape(double_width, double_width, double_width, double_width).astype(
        jnp.bfloat16
    )
    columns = lax.broadcasted_iota(jnp.int32, (1, X), 1)
    masked = jnp.where(columns < kept_ranks[0, 0], factors[0], jnp.zeros_like(factors[0]))
    left_factor = from_behind(masked, "cols", 1)
    own_front = fronts[0]
    right_view = masked.reshape(X, double_width, X)
    count_blocks = X // block_rows
    left_blocks = left_factor.reshape(X, double_width, count_blocks, block_rows).transpose(
        2, 0, 1, 3
    )

    def one_block(factor_block):
        projected = jnp.einsum(
            "xla,xvy->lavy", factor_block, own_front, preferred_element_type=jnp.float32
        ).astype(jnp.bfloat16)
        absorbed = jnp.einsum(
            "lavy,lvwq->awqy", projected, doubled, preferred_element_type=jnp.float32
        ).astype(jnp.bfloat16)
        return jnp.einsum(
            "awqy,yqb->awb", absorbed, right_view, preferred_element_type=jnp.float32
        ).astype(jnp.bfloat16)

    unscaled = lax.map(one_block, left_blocks).reshape(X, double_width, X)
    unscaled = lax.optimization_barrier(unscaled)
    local_top = jnp.max(jnp.abs(unscaled.astype(jnp.float32)))
    row_top = lax.pmax(local_top, "cols")
    normalized = (unscaled.astype(jnp.float32) / (row_top + epsilon)).astype(jnp.bfloat16)
    passed = partner(normalized, "rows", 0)
    return passed[None]


def solution(mesh):
    placed = (
        P("rows", None, None, "cols"),
        P("rows", None, "cols"),
        P("rows", None, "cols"),
        P("rows", None, "cols"),
        P("rows", "cols"),
    )
    return jax.shard_map(
        per_device,
        mesh=mesh,
        in_specs=placed,
        out_specs=P("rows", None, None, "cols"),
        check_vma=False,
    )
```

profile of v0, /device:TPU:24, one launch (start us, length us, event | category | flops | bytes accessed | tf_op | source)
XLA Modules:
  0.0 242.6 jit_solution(17241264479202851370)
XLA Ops:
  0.0 0.0 copy-start
  0.7 1.1 bitcast_select_fusion
  1.8 1.9 collective-permute-start
  3.7 0.8 reshape_squeeze.3
  4.5 0.8 reshape.33
  5.3 0.0 copy-done
  5.3 3.1 %fusion.18 = bf16[4,4,4,4,4,4,4,4]{7,3,6,5,4,2,1,0:T(4,128)(2,1)} fusion(f32[1,4,4]{2,1,0:T(4,128)S(1)} %copy-done, bf16[4,4,4,4,4]{4,3,2,1,0:T(4,128)(2,1)S(1)} %reshape_squeeze.3), kind=kOutput, calls=%fused_computation.24 | convolution fusion | flops 532480 | bytes 133184 | tf_op jit(solution)/shard_map/vlwqs,st,VLWQt->lLvVwWqQ/dot_general | solution.py:28
  8.4 5.9 %fusion.15 = bf16[4,4,4,4,4,4,4,4]{7,6,5,1,3,4,0,2:T(4,128)(2,1)} fusion(bf16[4,4,4,4,4,4,4,4]{7,3,6,5,4,2,1,0:T(4,128)(2,1)} %fusion.18, pred[]{:T(512)S(6)} %eq.5, bf16[4,4,4,4,4]{4,3,2,1,0:T(4,128)(2,1)S(1)} %reshape_squeeze.3, bf16[4,4,4,4,4,1,1,1]{4,3,2,1,0,5,6,7:T(4,128)(2,1)S(1)} %reshape.33, f32[1,4,4]{2,1,0:T(4,128)S(1)} %copy-done), kind=kOutput, calls=%fused_computation.17 | convolution fusion | flops 598016 | bytes 266305 | tf_op jit(solution)/shard_map/vlwqs,st,VLWQt->lLvVwWqQ/dot_general | solution.py:28
  14.3 6.6 %copy.8 = bf16[4,4,4,4,4,4,4,4]{7,6,5,4,3,2,1,0:T(4,128)(2,1)} copy(bf16[4,4,4,4,4,4,4,4]{7,6,5,1,3,4,0,2:T(4,128)(2,1)} %fusion.15) | data formatting | bytes 262144 | tf_op jit(solution)/shard_map/convert_element_type | solution.py:39
  21.0 0.0 copy-start.1
  21.0 5.3 %convert_element_type.30 = bf16[16,16,16,16]{3,2,1,0:T(8,128)(2,1)S(1)} reshape(bf16[4,4,4,4,4,4,4,4]{7,6,5,4,3,2,1,0:T(4,128)(2,1)} %copy.8) | data formatting | bytes 262144 | tf_op jit(solution)/shard_map/convert_element_type | solution.py:39
  26.2 0.0 copy-done.1
  26.3 0.9 copy.10
  27.2 0.0 collective-permute-done
  27.2 4.0 %reshape.20 = bf16[128,16,8,16]{3,2,1,0:T(8,128)(2,1)} reshape(bf16[2048,128]{1,0:T(8,128)(2,1)S(1)} %collective-permute-done) | data formatting | bytes 1048576 | tf_op jit(solution)/shard_map/reshape | solution.py:48
  31.2 6.1 %copy.9 = bf16[8,128,16,16]{1,3,2,0:T(8,128)(2,1)} copy(bf16[8,128,16,16]{3,0,2,1:T(8,128)(2,1)} %bitcast.128) | data formatting | bytes 1048576 | tf_op jit(solution)/shard_map/while | solution.py:63
  37.3 49.1 %while.10 = (s32[]{:T(128)}, bf16[8,16,16,128]{3,2,1,0:T(8,128)(2,1)}, bf16[8,128,16,16]{1,3,2,0:T(8,128)(2,1)}, bf16[128,16,128]{2,1,0:T(8,128)(2,1)}, bf16[16,...) while((s32[]{:T(128)}, bf16[8,16,16,128]{3,2,1,0:T(8,128)(2,1)}, ...), condition=%wide.region_1.2_spmd, body=%wide.region_0.1_spmd.sunk | while | flops 537427968 | bytes 3671117 | solution.py:63
  37.3 1.5 fusion.54
  38.8 2.0 copy.46
  40.8 2.7 %fusion.55 = bf16[8,16,16,128]{3,2,1,0:T(8,128)(2,1)} fusion(bf16[8,16,16,128]{3,2,1,0:T(8,128)(2,1)} %get-tuple-element.101, s32[]{:T(128)} %get-tuple-element.100, bf16[16,16,16,16,1]{2,1,0,3,4:T(8,128)(2,1)S(1)} %copy.46, bf16[128,16,128]{2,0,1:T(8,128)(2,1)} %get-tuple-element.112, bf16[16,16,16,128]{3,1,2,0:T(8,128)(2,1)S(1)} %fusion.54), kind=kOutput, calls=%fused_computation.7.clone.1 | convolution fusion | flops 403210240 | bytes 1769984 | tf_op jit(solution)/shard_map/while/body/eval_jaxpr/awqy,yqb->awb/dot_general | solution.py:59
  43.4 1.5 fusion.54
  45.0 2.0 copy.46
  46.9 2.6 %fusion.55 = bf16[8,16,16,128]{3,2,1,0:T(8,128)(2,1)} fusion(bf16[8,16,16,128]{3,2,1,0:T(8,128)(2,1)} %get-tuple-element.101, s32[]{:T(128)} %get-tuple-element.100, bf16[16,16,16,16,1]{2,1,0,3,4:T(8,128)(2,1)S(1)} %copy.46, bf16[128,16,128]{2,0,1:T(8,128)(2,1)} %get-tuple-element.112, bf16[16,16,16,128]{3,1,2,0:T(8,128)(2,1)S(1)} %fusion.54), kind=kOutput, calls=%fused_computation.7.clone.1 | convolution fusion | flops 403210240 | bytes 1769984 | tf_op jit(solution)/shard_map/while/body/eval_jaxpr/awqy,yqb->awb/dot_general | solution.py:59
  49.6 1.5 fusion.54
  51.1 2.0 copy.46
  53.1 2.6 %fusion.55 = bf16[8,16,16,128]{3,2,1,0:T(8,128)(2,1)} fusion(bf16[8,16,16,128]{3,2,1,0:T(8,128)(2,1)} %get-tuple-element.101, s32[]{:T(128)} %get-tuple-element.100, bf16[16,16,16,16,1]{2,1,0,3,4:T(8,128)(2,1)S(1)} %copy.46, bf16[128,16,128]{2,0,1:T(8,128)(2,1)} %get-tuple-element.112, bf16[16,16,16,128]{3,1,2,0:T(8,128)(2,1)S(1)} %fusion.54), kind=kOutput, calls=%fused_computation.7.clone.1 | convolution fusion | flops 403210240 | bytes 1769984 | tf_op jit(solution)/shard_map/while/body/eval_jaxpr/awqy,yqb->awb/dot_general | solution.py:59
  55.7 1.5 fusion.54
  57.2 2.0 copy.46
  59.2 2.6 %fusion.55 = bf16[8,16,16,128]{3,2,1,0:T(8,128)(2,1)} fusion(bf16[8,16,16,128]{3,2,1,0:T(8,128)(2,1)} %get-tuple-element.101, s32[]{:T(128)} %get-tuple-element.100, bf16[16,16,16,16,1]{2,1,0,3,4:T(8,128)(2,1)S(1)} %copy.46, bf16[128,16,128]{2,0,1:T(8,128)(2,1)} %get-tuple-element.112, bf16[16,16,16,128]{3,1,2,0:T(8,128)(2,1)S(1)} %fusion.54), kind=kOutput, calls=%fused_computation.7.clone.1 | convolution fusion | flops 403210240 | bytes 1769984 | tf_op jit(solution)/shard_map/while/body/eval_jaxpr/awqy,yqb->awb/dot_general | solution.py:59
  61.9 1.5 fusion.54
  63.4 2.0 copy.46
  65.3 2.6 %fusion.55 = bf16[8,16,16,128]{3,2,1,0:T(8,128)(2,1)} fusion(bf16[8,16,16,128]{3,2,1,0:T(8,128)(2,1)} %get-tuple-element.101, s32[]{:T(128)} %get-tuple-element.100, bf16[16,16,16,16,1]{2,1,0,3,4:T(8,128)(2,1)S(1)} %copy.46, bf16[128,16,128]{2,0,1:T(8,128)(2,1)} %get-tuple-element.112, bf16[16,16,16,128]{3,1,2,0:T(8,128)(2,1)S(1)} %fusion.54), kind=kOutput, calls=%fused_computation.7.clone.1 | convolution fusion | flops 403210240 | bytes 1769984 | tf_op jit(solution)/shard_map/while/body/eval_jaxpr/awqy,yqb->awb/dot_general | solution.py:59
  68.0 1.5 fusion.54
  69.5 2.0 copy.46
  71.5 2.6 %fusion.55 = bf16[8,16,16,128]{3,2,1,0:T(8,128)(2,1)} fusion(bf16[8,16,16,128]{3,2,1,0:T(8,128)(2,1)} %get-tuple-element.101, s32[]{:T(128)} %get-tuple-element.100, bf16[16,16,16,16,1]{2,1,0,3,4:T(8,128)(2,1)S(1)} %copy.46, bf16[128,16,128]{2,0,1:T(8,128)(2,1)} %get-tuple-element.112, bf16[16,16,16,128]{3,1,2,0:T(8,128)(2,1)S(1)} %fusion.54), kind=kOutput, calls=%fused_computation.7.clone.1 | convolution fusion | flops 403210240 | bytes 1769984 | tf_op jit(solution)/shard_map/while/body/eval_jaxpr/awqy,yqb->awb/dot_general | solution.py:59
  74.1 1.5 fusion.54
  75.6 2.0 copy.46
  77.6 2.6 %fusion.55 = bf16[8,16,16,128]{3,2,1,0:T(8,128)(2,1)} fusion(bf16[8,16,16,128]{3,2,1,0:T(8,128)(2,1)} %get-tuple-element.101, s32[]{:T(128)} %get-tuple-element.100, bf16[16,16,16,16,1]{2,1,0,3,4:T(8,128)(2,1)S(1)} %copy.46, bf16[128,16,128]{2,0,1:T(8,128)(2,1)} %get-tuple-element.112, bf16[16,16,16,128]{3,1,2,0:T(8,128)(2,1)S(1)} %fusion.54), kind=kOutput, calls=%fused_computation.7.clone.1 | convolution fusion | flops 403210240 | bytes 1769984 | tf_op jit(solution)/shard_map/while/body/eval_jaxpr/awqy,yqb->awb/dot_general | solution.py:59
  80.3 1.5 fusion.54
  81.8 2.0 copy.46
  83.8 2.6 %fusion.55 = bf16[8,16,16,128]{3,2,1,0:T(8,128)(2,1)} fusion(bf16[8,16,16,128]{3,2,1,0:T(8,128)(2,1)} %get-tuple-element.101, s32[]{:T(128)} %get-tuple-element.100, bf16[16,16,16,16,1]{2,1,0,3,4:T(8,128)(2,1)S(1)} %copy.46, bf16[128,16,128]{2,0,1:T(8,128)(2,1)} %get-tuple-element.112, bf16[16,16,16,128]{3,1,2,0:T(8,128)(2,1)S(1)} %fusion.54), kind=kOutput, calls=%fused_computation.7.clone.1 | convolution fusion | flops 403210240 | bytes 1769984 | tf_op jit(solution)/shard_map/while/body/eval_jaxpr/awqy,yqb->awb/dot_general | solution.py:59
  86.4 1.8 fusion.16
  88.2 140.7 %pmax.7 = f32[]{:T(128)} all-reduce(f32[]{:T(128)} %fusion.16), channel_id=1, replica_groups=mesh['rows'=8,'cols'=64] {'cols'}, use_global_device_ids=true, to_apply=%region_3.4 | all-reduce | flops 1 | bytes 8 | tf_op jit(solution)/shard_map/pmax | solution.py:66
  229.6 1.1 fusion.17
  230.8 1.9 collective-permute-start.1
  232.7 9.1 %collective-permute-done.1 = bf16[128,16,128]{2,1,0:T(8,128)(2,1)S(1)} collective-permute-done((bf16[128,16,128]{2,1,0:T(8,128)(2,1)S(1)}, bf16[128,16,128]{2,1,0:T(8,128)(2,1)S(1)}, u32[]{:S(2)}, u32[]{:S(2)}) %collective-permute-start.1) | collective-permute-done | bytes 524320 | tf_op jit(solution)/shard_map/ppermute | solution.py:24
  241.8 0.8 copy.58
  (3 shorter events, 0.0 us)
Async XLA Ops:
  0.0 5.3 %copy-start = (f32[1,4,4]{2,1,0:T(4,128)S(1)}, f32[1,4,4]{2,1,0:T(4,128)}, u32[]{:S(2)}) copy-start(f32[1,4,4]{2,1,0:T(4,128)} %param.10) | copy-start | bytes 196
  1.8 25.5 %collective-permute-start = (bf16[2048,128]{1,0:T(8,128)(2,1)S(1)}, bf16[2048,128]{1,0:T(8,128)(2,1)S(1)}, u32[]{:S(2)}, u32[]{:S(2)}) collective-permute-start(bf16[2048,128]{1,0:T(8,128)(2,1)S(1)} %bitcast_select_fusion), channel_id=1, source_target_pairs={{63,0},{0,1},{1,2},{2,3},{3,4},{4,5},{5,6},{6,7},{7,8},{8,9},{9,10... | collective-permute-start | bytes 1572872 | tf_op jit(solution)/shard_map/ppermute | solution.py:18
  21.0 5.3 %copy-start.1 = (bf16[1,2048,128]{2,1,0:T(8,128)(2,1)S(1)}, bf16[1,2048,128]{2,1,0:T(8,128)(2,1)}, u32[]{:S(2)}) copy-start(bf16[1,2048,128]{2,1,0:T(8,128)(2,1)} %param.8) | copy-start | bytes 1572868
  230.8 11.1 %collective-permute-start.1 = (bf16[128,16,128]{2,1,0:T(8,128)(2,1)S(1)}, bf16[128,16,128]{2,1,0:T(8,128)(2,1)S(1)}, u32[]{:S(2)}, u32[]{:S(2)}) collective-permute-start(bf16[128,16,128]{2,1,0:T(8,128)(2,1)S(1)} %fusion.17), channel_id=1, source_target_pairs={{0,64},{64,0},{128,192},{192,128},{256,320},{320,256},{384,448},{4... | collective-permute-start | bytes 1572872 | tf_op jit(solution)/shard_map/ppermute | solution.py:24
where the time goes:
time: 244 us; the launch traced here: 243 us
  blocking collectives  141 us (58%)
  matrix products  42.2 us (17%)
  local copies, waits for them, and re-layouts  41.1 us (17%)
  waiting for transfers between devices  9.15 us (4%)
  other arithmetic  4.07 us (2%)
  starting transfers between devices  3.84 us (2%)
    pmax x1, blocking collectives, per_device(): row_top = lax.pmax(local_top, 'cols')  141 us
    dot_general x8, matrix products, one_block(): jnp.einsum('awqy,yqb->awb', absorbed, right_view, preferred_element_type=...  21.2 us
    another operation x8, local copies, waits for them, and re-layouts  15.8 us
    dot_general x8, matrix products, one_block(): jnp.einsum('xla,xvy->lavy', factor_block, own_front, preferred_element_ty...  12 us
    convert_element_type x2, local copies, waits for them, and re-layouts, per_device(): doubled.reshape(double_width, double_width, double_width, double_width)  11.9 us
    ppermute x1, waiting for transfers between devices, partner(): return lax.ppermute(value, axis, pairs)  9.15 us
    dot_general x2, matrix products, double_layer(): return jnp.einsum('vlwqs,st,VLWQt->lLvVwWqQ', tensor, operator, tensor)  8.97 us
    while x2, local copies, waits for them, and re-layouts, per_device(): unscaled = lax.map(one_block, left_blocks).reshape(X, double_width, X)  6.98 us
  transfers between devices with their start and end apart: 2, of which 1 were waited for; matrix products, arithmetic and copies ran while one was open for 10% of the time, Pallas kernels for 0%

commit v1 on v0

v1 whole, which is shorter than its diff:
```python
import jax
import jax.numpy as jnp
from jax import lax
from jax.experimental import pallas as pl
from jax.experimental.pallas import tpu as pltpu
from jax.sharding import PartitionSpec as P

X = 128
D = 4
S = 4
D2 = D * D
TILE = D2 * D2
CHUNKS = X // D2
QUAD = 4
EPSILON = 1e-06

MESH = pl.DeviceIdType.MESH
BF16 = jnp.bfloat16
F32 = jnp.float32
NT = (((1,), (1,)), ((), ()))


def dot(a, b):
    return jnp.dot(a, b, preferred_element_type=F32)


def dot_nt(a, b):
    return lax.dot_general(a, b, NT, preferred_element_type=F32)


def iota(shape, dim):
    return lax.broadcasted_iota(jnp.int32, shape, dim)


def select(condition):
    return jnp.where(condition, 1.0, 0.0).astype(BF16)


def swap_16():
    rows, columns = iota((TILE, TILE), 0), iota((TILE, TILE), 1)
    return select(columns == (rows % D2) * D2 + rows // D2)


def double_layer(site, operators, odd):
    wide = jnp.concatenate([site, site], axis=1)
    rows, columns = iota(wide.shape, 0), iota(wide.shape, 1)
    shift = (rows // D - columns // D2 + 2 * D) % D
    swapped = jnp.where(shift == 0, wide, 0.0)
    for k in range(1, D):
        moved = pltpu.roll(pltpu.roll(wide, D * k, 0), wide.shape[1] - D2 * k, 1)
        swapped = jnp.where(shift == k, moved, swapped)
    wide = jnp.where(odd == 1, swapped, wide)
    half = D * D2
    high = wide.astype(BF16)
    low = (wide - high.astype(F32)).astype(BF16)
    parts = jnp.where(columns < half, high.astype(F32), low.astype(F32)).astype(BF16)
    index, entry = iota((TILE, D2), 0), iota((TILE, D2), 1)
    v_index, l_index = index // D2, index % D2
    ket_rows = select(entry == (v_index // D) * D + l_index // D)
    bra_rows = select(entry == (v_index % D) * D + l_index % D)
    ket = dot(ket_rows, parts).astype(BF16)
    bra = dot(bra_rows, parts).astype(BF16)
    index, entry = iota((TILE, 4 * half), 0), iota((TILE, 4 * half), 1)
    q_index, w_index = index // D2, index % D2
    ket_place = (w_index // D) * D2 + (q_index // D) * S
    bra_place = (w_index % D) * D2 + (q_index % D) * S
    ket_match = entry % half - entry % S == ket_place
    ket = jnp.concatenate([ket, ket], axis=1)
    lanes = iota((8, 4 * half), 1)
    total = None
    for t in range(S):
        column = jnp.zeros(lanes.shape, F32)
        for s in range(S):
            column = jnp.where(lanes % S == s, operators[s][t], column)
        high = column.astype(BF16).astype(F32)
        column = jnp.where(lanes < 2 * half, high, column - high)[:1]
        left = dot_nt(jnp.where(ket_match, column, 0.0).astype(BF16), ket)
        places = entry[:, : 2 * half] % half == bra_place[:, : 2 * half] + t
        term = left * dot_nt(select(places), bra)
        total = term if total is None else total + term
    return total.astype(BF16)


def kernel(
    n_columns,
    kept_ref,
    operator_hbm,
    site_hbm,
    front_hbm,
    factor_hbm,
    arrived_ref,
    divisor_ref,
    operator_ref,
    site_ref,
    front_ref,
    factor_ref,
    planes_ref,
    turned_ref,
    sent_ref,
    left_ref,
    front_planes_ref,
    doubled_ref,
    projected_a,
    projected_b,
    absorbed_a,
    absorbed_b,
    unscaled_ref,
    quad_ref,
    ring_ref,
    load_sem,
    left_send,
    left_recv,
    front_send,
    front_recv,
    quad_send,
    quad_recv,
    ring_send,
    ring_recv,
    top_send,
    top_recv,
):
    n_ring = n_columns // QUAD
    row, column = lax.axis_index("rows"), lax.axis_index("cols")
    odd = lax.rem(row, 2)
    partner = row + 1 - 2 * odd
    before = lax.rem(column + n_columns - 1, n_columns)
    behind = lax.rem(column + 1, n_columns)
    place, member = column // QUAD, lax.rem(column, QUAD)

    def load(source, target, k):
        copy = pltpu.make_async_copy(source, target, load_sem.at[k])
        copy.start()
        return copy

    load_factor = load(factor_hbm, factor_ref, 0)
    load_front = load(front_hbm, front_ref, 1)
    load_site = load(site_hbm, site_ref, 2)
    load_operator = load(operator_hbm, operator_ref, 3)

    barrier = pltpu.get_barrier_semaphore()

    def greet(to_row, to_column):
        pl.semaphore_signal(barrier, inc=1, device_id=(to_row, to_column), device_id_type=MESH)

    def quad_column(k):
        return place * QUAD + lax.rem(member + k, QUAD)

    def ring_column(k):
        return lax.rem(place + k, n_ring) * QUAD + member

    greet(row, before)
    greet(row, behind)
    greet(partner, column)
    for k in range(1, QUAD):
        greet(row, quad_column(k))

    def greet_ring(k, carry):
        greet(row, ring_column(k))
        return carry

    lax.fori_loop(1, n_ring, greet_ring, 0)

    def chunk(ref, i):
        return ref.at[pl.ds(pl.multiple_of(i * TILE, TILE), TILE), :]

    def beside(ref, i):
        return jnp.concatenate(
            [ref[i * TILE : (i + 1) * TILE, :], ref[(i + 1) * TILE : (i + 2) * TILE, :]], axis=1
        )

    swap = swap_16()
    identity = select(iota((X, X), 0) == iota((X, X), 1))
    kept_columns = iota((TILE, 2 * X), 1) % X < kept_ref[0, 0]
    load_factor.wait()

    for i in range(0, CHUNKS, 2):
        both = jnp.where(kept_columns, dot(swap, beside(factor_ref, i)), 0.0).astype(BF16)
        for k in range(2):
            for q in range(D2):
                start = q * X + (i + k) * D2
                planes_ref[start : start + D2, :] = both[
                    q * D2 : (q + 1) * D2, k * X : (k + 1) * X
                ]

    for q in range(0, D2, 2):
        both = dot_nt(identity, planes_ref[q * X : (q + 2) * X, :]).astype(BF16)
        for k in range(2):
            for i in range(CHUNKS):
                start = i * TILE + (q + k) * D2
                turned_ref[start : start + D2, :] = both[
                    i * D2 : (i + 1) * D2, k * X : (k + 1) * X
                ]

    for i in range(0, CHUNKS, 2):
        both = dot(swap, beside(turned_ref, i)).astype(BF16)
        for k in range(2):
            sent_ref[(i + k) * TILE : (i + k + 1) * TILE, :] = both[:, k * X : (k + 1) * X]

    pl.semaphore_wait(barrier, 2 + 1 + (QUAD - 1) + (n_ring - 1))

    def left_copy(i):
        return pltpu.make_async_remote_copy(
            src_ref=chunk(sent_ref, i),
            dst_ref=chunk(left_ref, i),
            send_sem=left_send.at[i],
            recv_sem=left_recv.at[i],
            device_id=(row, behind),
            device_id_type=MESH,
        )

    def start_left(i, carry):
        left_copy(i).start()
        return carry

    lax.fori_loop(0, CHUNKS, start_left, 0)

    load_front.wait()
    for i in range(0, CHUNKS, 2):
        both = dot(swap, beside(front_ref, i)).astype(BF16)
        for k in range(2):
            for v in range(D2):
                front_planes_ref[(i + k) * D2 : (i + k + 1) * D2, v * X : (v + 1) * X] = both[
                    v * D2 : (v + 1) * D2, k * X : (k + 1) * X
                ]

    load_site.wait()
    load_operator.wait()
    doubled_ref[...] = double_layer(
        site_ref[0], [[operator_ref[0, s, t] for t in range(S)] for s in range(S)], odd
    )

    def front_copy(i):
        return pltpu.make_async_remote_copy(
            src_ref=chunk(unscaled_ref, i),
            dst_ref=chunk(arrived_ref, i),
            send_sem=front_send.at[i],
            recv_sem=front_recv.at[i],
            device_id=(partner, column),
            device_id_type=MESH,
        )

    def finish_chunk(absorbed_ref, i, top):
        result = dot(absorbed_ref[...], planes_ref[...])
        unscaled_ref[pl.ds(pl.multiple_of(i * TILE, TILE), TILE), :] = result.astype(BF16)
        front_copy(i).start()
        return jnp.maximum(top, jnp.max(jnp.abs(result).reshape(TILE // 8, 8, X), axis=0))

    def project(left, projected_ref, v):
        both = dot(left, front_planes_ref[:, v * X : (v + 2) * X]).astype(BF16)
        for k in range(2):
            projected_ref[:, (v + k) * D2 : (v + k + 1) * D2, :] = both[
                :, k * X : (k + 1) * X
            ].reshape(D2, D2, X)

    def absorb(projected_ref, absorbed_ref, a):
        pair = jnp.concatenate([projected_ref[a], projected_ref[a + 1]], axis=1)
        both = dot(doubled_ref[...], pair).astype(BF16)
        for k in range(2):
            for q in range(D2):
                absorbed_ref[(a + k) * D2 : (a + k + 1) * D2, q * X : (q + 1) * X] = both[
                    q * D2 : (q + 1) * D2, k * X : (k + 1) * X
                ]

    def step(i, even, top, first=True, middle=True, last=True):
        projected = (projected_a, projected_b) if even else (projected_b, projected_a)
        absorbed = (absorbed_a, absorbed_b) if even else (absorbed_b, absorbed_a)
        if last:
            top = finish_chunk(absorbed[1], i - 1, top)
        if first:
            left_copy(i + 1).wait_recv()
            left = left_ref[pl.ds(pl.multiple_of((i + 1) * TILE, TILE), TILE), :]
        for k in range(0, D2, 2):
            if first:
                project(left, projected[1], k)
            if middle:
                absorb(projected[0], absorbed[0], k)
        return top

    def two_steps(n, top):
        return step(2 * n + 2, True, step(2 * n + 1, False, top))

    top = jnp.zeros((8, X), F32)
    step(-1, False, top, middle=False, last=False)
    step(0, True, top, last=False)
    top = lax.fori_loop(0, (CHUNKS - 2) // 2, two_steps, top)
    top = step(CHUNKS - 1, False, top, first=False)
    top = step(CHUNKS, True, top, first=False, middle=False)
    top = top.astype(BF16).astype(F32)

    def quad_copy(k):
        return pltpu.make_async_remote_copy(
            src_ref=quad_ref.at[member],
            dst_ref=quad_ref.at[member],
            send_sem=quad_send.at[k],
            recv_sem=quad_recv.at[member],
            device_id=(row, quad_column(k)),
            device_id_type=MESH,
        )

    def arrival(ref, sems, slot):
        return pltpu.make_async_remote_copy(
            src_ref=ref.at[slot],
            dst_ref=ref.at[slot],
            send_sem=sems.at[slot],
            recv_sem=sems.at[slot],
            device_id=(row, behind),
            device_id_type=MESH,
        )

    quad_ref[member] = top
    for k in range(1, QUAD):
        quad_copy(k).start()
    for k in range(1, QUAD):
        arrival(quad_ref, quad_recv, lax.rem(member + k, QUAD)).wait_recv()
    for k in range(1, QUAD):
        quad_copy(k).wait_send()
    ring_ref[place] = jnp.max(quad_ref[:QUAD], axis=0)

    def ring_copy(k):
        return pltpu.make_async_remote_copy(
            src_ref=ring_ref.at[place],
            dst_ref=ring_ref.at[place],
            send_sem=ring_send.at[k],
            recv_sem=ring_recv.at[place],
            device_id=(row, ring_column(k)),
            device_id_type=MESH,
        )

    def start_ring(k, carry):
        ring_copy(k).start()
        return carry

    def end_ring(k, carry):
        arrival(ring_ref, ring_recv, lax.rem(place + k, n_ring)).wait_recv()
        ring_copy(k).wait_send()
        return carry

    lax.fori_loop(1, n_ring, start_ring, 0)
    lax.fori_loop(1, n_ring, end_ring, 0)

    own_top = quad_ref.at[QUAD]
    own_top[...] = jnp.broadcast_to(jnp.max(ring_ref[...]), (8, X))
    top_copy = pltpu.make_async_remote_copy(
        src_ref=own_top,
        dst_ref=quad_ref.at[QUAD + 1],
        send_sem=top_send,
        recv_sem=top_recv,
        device_id=(partner, column),
        device_id_type=MESH,
    )
    top_copy.start()
    top_copy.wait_recv()
    divisor_ref[...] = quad_ref[QUAD + 1, :1, :1] + EPSILON

    def finish(i, carry):
        left_copy(i).wait_send()
        front_copy(i).wait()
        return carry

    lax.fori_loop(0, CHUNKS, finish, 0)
    top_copy.wait_send()


def per_device(fronts, factors, site_tensors, operators, kept_ranks):
    n_columns = lax.axis_size("cols")
    rows = X * D2
    smem = pl.BlockSpec(memory_space=pltpu.SMEM)
    hbm = pl.BlockSpec(memory_space=pltpu.HBM)
    vmem = pl.BlockSpec(memory_space=pltpu.VMEM)
    anywhere = pl.BlockSpec(memory_space=pl.ANY)
    dma = pltpu.SemaphoreType.DMA

    def body(*refs):
        kernel(n_columns, *refs)

    flops = 2 * 4 * X * X * X * D2 * D2
    arrived, divisor = pl.pallas_call(
        body,
        out_shape=(
            jax.ShapeDtypeStruct((rows, X), BF16),
            jax.ShapeDtypeStruct((1, 1), F32),
        ),
        in_specs=[smem] + [hbm] * 4,
        out_specs=(anywhere, vmem),
        scratch_shapes=[
            pltpu.SMEM(operators.shape, F32),
            pltpu.VMEM(site_tensors.shape, F32),
            pltpu.VMEM((rows, X), BF16),
            pltpu.VMEM((rows, X), BF16),
            pltpu.VMEM((rows, X), BF16),
            pltpu.VMEM((rows, X), BF16),
            pltpu.VMEM((rows, X), BF16),
            pltpu.VMEM((rows, X), BF16),
            pltpu.VMEM((X, rows), BF16),
            pltpu.VMEM((TILE, TILE), BF16),
            pltpu.VMEM((D2, TILE, X), BF16),
            pltpu.VMEM((D2, TILE, X), BF16),
            pltpu.VMEM((TILE, rows), BF16),
            pltpu.VMEM((TILE, rows), BF16),
            pltpu.VMEM((rows, X), BF16),
            pltpu.VMEM((QUAD + 2, 8, X), F32),
            pltpu.VMEM((n_columns // QUAD, 8, X), F32),
            dma((4,)),
            dma((CHUNKS,)),
            dma((CHUNKS,)),
            dma((CHUNKS,)),
            dma((CHUNKS,)),
            dma((QUAD,)),
            dma((QUAD,)),
            dma((n_columns // QUAD,)),
            dma((n_columns // QUAD,)),
            dma,
            dma,
        ],
        compiler_params=pltpu.CompilerParams(
            collective_id=0, has_side_effects=True, vmem_limit_bytes=40 * 2**20
        ),
        cost_estimate=pl.CostEstimate(flops=flops, bytes_accessed=3 * 2**19, transcendentals=0),
    )(
        kept_ranks,
        *(
            pltpu.with_memory_space_constraint(operand, pltpu.HBM)
            for operand in (
                operators,
                site_tensors,
                fronts.reshape(rows, X),
                factors.reshape(rows, X),
            )
        )
    )
    normalized = arrived.astype(F32) / divisor[0, 0]
    return normalized.astype(BF16).reshape(1, X, D2, X)


def solution(mesh):
    return jax.shard_map(
        per_device,
        mesh=mesh,
        in_specs=(
            P("rows", None, None, "cols"),
            P("rows", None, "cols"),
            P("rows", None, "cols"),
            P("rows", None, "cols"),
            P("rows", "cols"),
        ),
        out_specs=P("rows", None, None, "cols"),
        check_vma=False,
    )
```

time: 244 us -> 45.2 us (0.19)
  the two profiles are of different devices: /device:TPU:24 before, /device:TPU:6 now
where the time goes in v1:
time: 45.2 us; the launch traced here: 45.1 us
  Pallas kernels  43 us (95%)
  other arithmetic  1.46 us (3%)
  between operations  0.66 us (1%)
    pallas_call x1, Pallas kernels, per_device(): pl.pallas_call(body, out_shape=(jax.ShapeDtypeStruct((rows, X), BF16), ja...  43 us
    convert_element_type x1, other arithmetic, per_device(): return normalized.astype(BF16).reshape(1, X, D2, X)  1.46 us

profile of v1, /device:TPU:6, one launch (start us, length us, event | category | flops | bytes accessed | tf_op | source)
XLA Modules:
  0.0 45.1 jit_solution(17931067637798933927)
XLA Ops:
  0.7 43.0 %shard_map.55 = (bf16[2048,128]{1,0:T(8,128)(2,1)S(1)}, f32[1,1]{1,0:T(1,128)}) custom-call(s32[1,1]{1,0:T(1,128)S(6)} %copy.6.refs_0_, f32[1,4,4]{2,1,0:T(4,128)} %refs_1_.1, f32[1,16,64]{2,1,0:T(8,128)} %refs_2_.1, bf16[2048,128]{1,0:T(8,128)(2,1)} %bitcast.4, bf16[2048,128]{1,0:T(8,128)(2,1)} %bitcast.5), custom_call_target="tpu_custom_call" | custom-call | flops 4294967296 | bytes 1572864 | tf_op jit(solution)/shard_map/pallas_call | solution.py:377
  43.6 1.5 %divide_convert_fusion = bf16[2048,128]{1,0:T(8,128)(2,1)} fusion(bf16[2048,128]{1,0:T(8,128)(2,1)S(1)} %get-tuple-element.7, f32[]{:T(128)} %bitcast.2), kind=kLoop, calls=%fused_computation | loop fusion | flops 786432 | bytes 1048580 | tf_op jit(solution)/shard_map/convert_element_type | solution.py:432

commit v2 on v1

v2 whole, which is shorter than its diff:
```python
import jax
import jax.numpy as jnp
from jax import lax
from jax.experimental import pallas as pl
from jax.experimental.pallas import tpu as pltpu
from jax.sharding import PartitionSpec as P

X = 128
D = 4
S = 4
D2 = D * D
TILE = D2 * D2
CHUNKS = X // D2
QUAD = 4
EPSILON = 1e-06

MESH = pl.DeviceIdType.MESH
BF16 = jnp.bfloat16
F32 = jnp.float32
NT = (((1,), (1,)), ((), ()))


def dot(a, b):
    return jnp.dot(a, b, preferred_element_type=F32)


def dot_nt(a, b):
    return lax.dot_general(a, b, NT, preferred_element_type=F32)


def iota(shape, dim):
    return lax.broadcasted_iota(jnp.int32, shape, dim)


def select(condition):
    return jnp.where(condition, 1.0, 0.0).astype(BF16)


def swap_16():
    rows, columns = iota((TILE, TILE), 0), iota((TILE, TILE), 1)
    return select(columns == ((rows & 15) << 4 | rows >> 4))


def double_layer(site, operator_ref, odd, ket_ref, bra_ref, total_ref):
    wide = jnp.concatenate([site, site], axis=1)
    rows, columns = iota(wide.shape, 0), iota(wide.shape, 1)
    shift = ((rows >> 2) - (columns >> 4)) & 3
    swapped = jnp.where(shift == 0, wide, 0.0)
    for k in range(1, D):
        moved = pltpu.roll(pltpu.roll(wide, D * k, 0), wide.shape[1] - D2 * k, 1)
        swapped = jnp.where(shift == k, moved, swapped)
    wide = jnp.where(odd == 1, swapped, wide)
    half = D * D2
    high = wide.astype(BF16)
    low = (wide - high.astype(F32)).astype(BF16)
    parts = jnp.where(columns < half, high.astype(F32), low.astype(F32)).astype(BF16)
    index, entry = iota((TILE, D2), 0), iota((TILE, D2), 1)
    ket_rows = select(entry == ((index >> 4 & 12) | (index >> 2 & 3)))
    bra_rows = select(entry == ((index >> 2 & 12) | (index & 3)))
    ket = dot(ket_rows, parts).astype(BF16)
    bra = dot(bra_rows, parts).astype(BF16)
    ket_ref[:, : 2 * half] = ket
    ket_ref[:, 2 * half :] = ket
    bra_ref[...] = bra
    total_ref[...] = jnp.zeros_like(total_ref)

    def add(t, carry):
        index, entry = iota((TILE, 4 * half), 0), iota((TILE, 4 * half), 1)
        ket_place = (index & 12) << 2 | (index >> 6) << 2
        bra_place = (index & 3) << 4 | (index >> 2 & 12)
        lanes = iota((8, 4 * half), 1)
        column = jnp.zeros(lanes.shape, F32)
        for s in range(S):
            column = jnp.where((lanes & 3) == s, operator_ref[0, s, t], column)
        high = column.astype(BF16).astype(F32)
        column = jnp.where(lanes < 2 * half, high, column - high)[:1]
        kets = jnp.where((entry & 60) == ket_place, column, 0.0).astype(BF16)
        bras = select((entry & 63) == bra_place + t)[:, : 2 * half]
        total_ref[...] += dot_nt(kets, ket_ref[...]) * dot_nt(bras, bra_ref[...])
        return carry

    lax.fori_loop(0, S, add, 0)
    return total_ref[...].astype(BF16)


def kernel(
    n_rows,
    n_columns,
    kept_ref,
    operator_hbm,
    site_hbm,
    front_hbm,
    factor_hbm,
    arrived_ref,
    divisor_ref,
    operator_ref,
    site_ref,
    front_ref,
    factor_ref,
    planes_ref,
    turned_ref,
    sent_ref,
    left_ref,
    relay_ref,
    front_planes_ref,
    swap_ref,
    identity_ref,
    ket_ref,
    bra_ref,
    total_ref,
    doubled_ref,
    projected_ref,
    absorbed_ref,
    unscaled_ref,
    quad_ref,
    ring_ref,
    load_sem,
    left_send,
    left_recv,
    relay_send,
    relay_recv,
    front_send,
    front_recv,
    quad_send,
    quad_recv,
    ring_send,
    ring_recv,
):
    n_ring = n_columns // QUAD
    row, column = lax.axis_index("rows"), lax.axis_index("cols")
    odd = lax.rem(row, 2)
    partner = row + 1 - 2 * odd
    before = lax.rem(column + n_columns - 1, n_columns)
    behind = lax.rem(column + 1, n_columns)
    place, member = column // QUAD, lax.rem(column, QUAD)
    core = lax.rem(column, 2)

    def beside_x(to_row, to_column, up):
        low = to_row // (n_rows // 2)
        flip = low if up else 1 - low
        start = (to_column // QUAD) * QUAD
        high = lax.rem(to_column, QUAD) // 2
        high = high + flip * (1 - 2 * high)
        return to_row + (n_rows // 2) * (1 - 2 * low), start + 2 * high + 1

    def load(source, target, k):
        copy = pltpu.make_async_copy(source, target, load_sem.at[k])
        copy.start()
        return copy

    load_factor = load(factor_hbm, factor_ref, 0)
    load_front = load(front_hbm, front_ref, 1)
    load_site = load(site_hbm, site_ref, 2)
    load_operator = load(operator_hbm, operator_ref, 3)

    barrier = pltpu.get_barrier_semaphore()

    def greet(to_row, to_column):
        pl.semaphore_signal(barrier, inc=1, device_id=(to_row, to_column), device_id_type=MESH)

    def quad_column(k):
        return place * QUAD + lax.rem(member + k, QUAD)

    def ring_column(k):
        return lax.rem(place + k, n_ring) * QUAD + member

    greet(row, before)
    greet(row, behind)
    greet(partner, column)
    for k in range(1, QUAD):
        greet(row, quad_column(k))

    def greet_ring(k, carry):
        greet(partner, ring_column(k))
        return carry

    lax.fori_loop(1, n_ring, greet_ring, 0)

    relay = beside_x(row, column, 0)
    served = beside_x(row, column, 1)
    served_target = served[0], lax.rem(served[1] + 1, n_columns)
    left_relay = beside_x(row, before, 0)

    @pl.when(core == 1)
    def _():
        greet(*served)

    @pl.when(core == 0)
    def _():
        greet(*left_relay)

    def chunk(ref, i):
        return ref.at[pl.ds(pl.multiple_of(i * TILE, TILE), TILE), :]

    def rows_of(i, size):
        return pl.ds(pl.multiple_of(i * size, size), size)

    def beside(ref, i):
        block = ref[rows_of(i, 2 * TILE), :]
        return jnp.concatenate([block[:TILE], block[TILE:]], axis=1)

    swap_ref[...] = swap_16()
    identity_ref[...] = select(iota((X, X), 0) == iota((X, X), 1))
    load_factor.wait()
    load_front.wait()

    def permute(i, carry):
        kept = (iota((TILE, 2 * X), 1) & (X - 1)) < kept_ref[0, 0]
        block = dot(swap_ref[...], beside(factor_ref, i))
        block = jnp.where(kept, block, 0.0).astype(BF16)
        other = dot(swap_ref[...], beside(front_ref, i)).astype(BF16)
        for k in range(2):
            lanes = slice(k * X, (k + 1) * X)
            for q in range(D2):
                start = pl.multiple_of(q * X + i * 2 * D2 + k * D2, D2)
                planes_ref[pl.ds(start, D2), :] = block[q * D2 : (q + 1) * D2, lanes]
            for v in range(D2):
                start = pl.multiple_of(i * 2 * D2 + k * D2, D2)
                front_planes_ref[pl.ds(start, D2), v * X : (v + 1) * X] = other[
                    v * D2 : (v + 1) * D2, lanes
                ]
        return carry

    lax.fori_loop(0, CHUNKS // 2, permute, 0)

    def turn(i, carry):
        for n in range(2):
            block = planes_ref[rows_of(2 * i + n, 2 * X), :]
            both = dot_nt(identity_ref[...], block).astype(BF16)
            for k in range(2):
                for j in range(CHUNKS):
                    start = pl.multiple_of(j * TILE + (4 * i + 2 * n + k) * D2, D2)
                    turned_ref[pl.ds(start, D2), :] = both[
                        j * D2 : (j + 1) * D2, k * X : (k + 1) * X
                    ]
        return carry

    lax.fori_loop(0, D2 // 4, turn, 0)

    def interleave(i, carry):
        for n in range(2):
            both = dot(swap_ref[...], beside(turned_ref, 2 * i + n)).astype(BF16)
            for k in range(2):
                sent_ref[rows_of(4 * i + 2 * n + k, TILE), :] = both[:, k * X : (k + 1) * X]
        return carry

    lax.fori_loop(0, CHUNKS // 4, interleave, 0)

    pl.semaphore_wait(barrier, 2 + 1 + (QUAD - 1) + (n_ring - 1) + 2 * core)

    def left_copy(i):
        return pltpu.make_async_remote_copy(
            src_ref=chunk(sent_ref, i),
            dst_ref=chunk(left_ref, i),
            send_sem=left_send.at[i],
            recv_sem=left_recv.at[i],
            device_id=(row, behind),
            device_id_type=MESH,
        )

    def relay_copy(i):
        return pltpu.make_async_remote_copy(
            src_ref=chunk(sent_ref, i),
            dst_ref=chunk(relay_ref, i // 2),
            send_sem=left_send.at[i],
            recv_sem=relay_recv.at[i // 2],
            device_id=relay,
            device_id_type=MESH,
        )

    def onward_copy(i):
        return pltpu.make_async_remote_copy(
            src_ref=chunk(relay_ref, i // 2),
            dst_ref=chunk(left_ref, i),
            send_sem=relay_send.at[i // 2],
            recv_sem=left_recv.at[i],
            device_id=served_target,
            device_id_type=MESH,
        )

    def send_left(i):
        left_copy(i).start()
        relay_copy(i + 1).start()

    def pass_on(i):
        relay_copy(i).wait_recv()
        onward_copy(i).start()

    def start_left(i, carry):
        left_copy(i).start()
        return carry

    @pl.when(core == 0)
    def _():
        lax.fori_loop(0, CHUNKS, start_left, 0)

    @pl.when(core == 1)
    def _():
        send_left(0)

    load_site.wait()
    load_operator.wait()
    doubled_ref[...] = double_layer(site_ref[0], operator_ref, odd, ket_ref, bra_ref, total_ref)

    @pl.when(core == 1)
    def _():
        send_left(2)
        pass_on(1)

    def front_copy(i):
        return pltpu.make_async_remote_copy(
            src_ref=chunk(unscaled_ref, i),
            dst_ref=chunk(arrived_ref, i),
            send_sem=front_send.at[i],
            recv_sem=front_recv.at[i],
            device_id=(partner, column),
            device_id_type=MESH,
        )

    def project(i):
        left = left_ref[rows_of(i, TILE), :]
        for v in range(0, D2, 2):
            both = dot(left, front_planes_ref[:, v * X : (v + 2) * X]).astype(BF16)
            for k in range(2):
                projected_ref[:, (v + k) * D2 : (v + k + 1) * D2, :] = both[
                    :, k * X : (k + 1) * X
                ].reshape(D2, D2, X)

    def absorb():
        for a in range(0, D2, 2):
            pair = jnp.concatenate([projected_ref[a], projected_ref[a + 1]], axis=1)
            both = dot(doubled_ref[...], pair).astype(BF16)
            for k in range(2):
                for q in range(D2):
                    absorbed_ref[(a + k) * D2 : (a + k + 1) * D2, q * X : (q + 1) * X] = both[
                        q * D2 : (q + 1) * D2, k * X : (k + 1) * X
                    ]

    def work(i, top):
        @pl.when(i < CHUNKS - 1)
        def _():
            left_copy(i + 1).wait_recv()

        @pl.when((core == 1) & (i < CHUNKS // 2 - 2))
        def _():
            send_left(2 * i + 4)

        @pl.when((core == 1) & (i >= 1) & (i < CHUNKS // 2))
        def _():
            pass_on(2 * i + 1)

        absorb()
        project(jnp.minimum(i + 1, CHUNKS - 1))
        result = dot(absorbed_ref[...], planes_ref[...])
        unscaled_ref[rows_of(i, TILE), :] = result.astype(BF16)
        front_copy(i).start()
        return jnp.maximum(top, jnp.max(jnp.abs(result).reshape(TILE // 8, 8, X), axis=0))

    left_copy(0).wait_recv()
    project(0)
    top = lax.fori_loop(0, CHUNKS, work, jnp.zeros((8, X), F32))
    top = jnp.max(top, axis=0, keepdims=True).astype(BF16).astype(F32)

    def quad_copy(k):
        return pltpu.make_async_remote_copy(
            src_ref=quad_ref.at[member],
            dst_ref=quad_ref.at[member],
            send_sem=quad_send.at[k],
            recv_sem=quad_recv.at[member],
            device_id=(row, quad_column(k)),
            device_id_type=MESH,
        )

    def arrival(ref, sems, slot):
        return pltpu.make_async_remote_copy(
            src_ref=ref.at[slot],
            dst_ref=ref.at[slot],
            send_sem=sems.at[slot],
            recv_sem=sems.at[slot],
            device_id=(row, behind),
            device_id_type=MESH,
        )

    quad_ref[member] = top
    for k in range(1, QUAD):
        quad_copy(k).start()
    for k in range(1, QUAD):
        arrival(quad_ref, quad_recv, lax.rem(member + k, QUAD)).wait_recv()
    for k in range(1, QUAD):
        quad_copy(k).wait_send()
    ring_ref[n_ring] = jnp.max(quad_ref[...], axis=0)

    def ring_copy(k):
        return pltpu.make_async_remote_copy(
            src_ref=ring_ref.at[n_ring],
            dst_ref=ring_ref.at[place],
            send_sem=ring_send.at[k],
            recv_sem=ring_recv.at[place],
            device_id=(partner, ring_column(k)),
            device_id_type=MESH,
        )

    def start_ring(k, carry):
        ring_copy(k).start()
        return carry

    def end_ring(k, carry):
        arrival(ring_ref, ring_recv, lax.rem(place + k, n_ring)).wait_recv()
        ring_copy(k).wait_send()
        return carry

    lax.fori_loop(0, n_ring, start_ring, 0)
    lax.fori_loop(0, n_ring, end_ring, 0)
    largest = jnp.max(ring_ref[:n_ring], axis=0)
    divisor_ref[...] = jnp.max(largest, axis=1, keepdims=True) + EPSILON

    def finish(i, carry):
        left_copy(i).wait_send()
        front_copy(i).wait()
        return carry

    lax.fori_loop(0, CHUNKS, finish, 0)

    @pl.when(core == 1)
    def _():
        for i in range(1, CHUNKS, 2):
            onward_copy(i).wait_send()


def per_device(fronts, factors, site_tensors, operators, kept_ranks):
    n_rows, n_columns = lax.axis_size("rows"), lax.axis_size("cols")
    rows = X * D2
    smem = pl.BlockSpec(memory_space=pltpu.SMEM)
    hbm = pl.BlockSpec(memory_space=pltpu.HBM)
    vmem = pl.BlockSpec(memory_space=pltpu.VMEM)
    anywhere = pl.BlockSpec(memory_space=pl.ANY)
    dma = pltpu.SemaphoreType.DMA

    def body(*refs):
        kernel(n_rows, n_columns, *refs)

    flops = 2 * 4 * X * X * X * D2 * D2
    arrived, divisor = pl.pallas_call(
        body,
        out_shape=(
            jax.ShapeDtypeStruct((rows, X), BF16),
            jax.ShapeDtypeStruct((1, 1), F32),
        ),
        in_specs=[smem] + [hbm] * 4,
        out_specs=(anywhere, vmem),
        scratch_shapes=[
            pltpu.SMEM(operators.shape, F32),
            pltpu.VMEM(site_tensors.shape, F32),
            pltpu.VMEM((rows, X), BF16),
            pltpu.VMEM((rows, X), BF16),
            pltpu.VMEM((rows, X), BF16),
            pltpu.VMEM((rows, X), BF16),
            pltpu.VMEM((rows, X), BF16),
            pltpu.VMEM((rows, X), BF16),
            pltpu.VMEM((rows // 2, X), BF16),
            pltpu.VMEM((X, rows), BF16),
            pltpu.VMEM((TILE, TILE), BF16),
            pltpu.VMEM((X, X), BF16),
            pltpu.VMEM((TILE, TILE), BF16),
            pltpu.VMEM((TILE, X), BF16),
            pltpu.VMEM((TILE, TILE), F32),
            pltpu.VMEM((TILE, TILE), BF16),
            pltpu.VMEM((D2, TILE, X), BF16),
            pltpu.VMEM((TILE, rows), BF16),
            pltpu.VMEM((rows, X), BF16),
            pltpu.VMEM((QUAD, 1, X), F32),
            pltpu.VMEM((n_columns // QUAD + 1, 1, X), F32),
            dma((4,)),
            dma((CHUNKS,)),
            dma((CHUNKS,)),
            dma((CHUNKS // 2,)),
            dma((CHUNKS // 2,)),
            dma((CHUNKS,)),
            dma((CHUNKS,)),
            dma((QUAD,)),
            dma((QUAD,)),
            dma((n_columns // QUAD,)),
            dma((n_columns // QUAD,)),
        ],
        compiler_params=pltpu.CompilerParams(
            collective_id=0, has_side_effects=True, vmem_limit_bytes=40 * 2**20
        ),
        cost_estimate=pl.CostEstimate(flops=flops, bytes_accessed=3 * 2**19, transcendentals=0),
    )(
        kept_ranks,
        *(
            pltpu.with_memory_space_constraint(operand, pltpu.HBM)
            for operand in (
                operators,
                site_tensors,
                fronts.reshape(rows, X),
                factors.reshape(rows, X),
            )
        )
    )
    normalized = arrived.astype(F32) / divisor[0, 0]
    return normalized.astype(BF16).reshape(1, X, D2, X)


def solution(mesh):
    return jax.shard_map(
        per_device,
        mesh=mesh,
        in_specs=(
            P("rows", None, None, "cols"),
            P("rows", None, "cols"),
            P("rows", None, "cols"),
            P("rows", None, "cols"),
            P("rows", "cols"),
        ),
        out_specs=P("rows", None, None, "cols"),
        check_vma=False,
    )
```

time: 45.2 us -> 44.6 us (0.987)
  the two profiles are of different devices: /device:TPU:6 before, /device:TPU:1 now
where the time goes in v2:
time: 44.6 us; the launch traced here: 44.5 us
  Pallas kernels  42.4 us (95%)
  other arithmetic  1.46 us (3%)
  between operations  0.66 us (1%)
    pallas_call x1, Pallas kernels, per_device(): pl.pallas_call(body, out_shape=(jax.ShapeDtypeStruct((rows, X), BF16), ja...  42.4 us
    convert_element_type x1, other arithmetic, per_device(): return normalized.astype(BF16).reshape(1, X, D2, X)  1.46 us

profile of v2, /device:TPU:1, one launch (start us, length us, event | category | flops | bytes accessed | tf_op | source)
XLA Modules:
  0.0 44.5 jit_solution(6118904609973389622)
XLA Ops:
  0.7 42.4 %shard_map.55 = (bf16[2048,128]{1,0:T(8,128)(2,1)S(1)}, f32[1,1]{1,0:T(1,128)}) custom-call(s32[1,1]{1,0:T(1,128)S(6)} %copy.6.refs_0_, f32[1,4,4]{2,1,0:T(4,128)} %refs_1_.1, f32[1,16,64]{2,1,0:T(8,128)} %refs_2_.1, bf16[2048,128]{1,0:T(8,128)(2,1)} %bitcast.4, bf16[2048,128]{1,0:T(8,128)(2,1)} %bitcast.5), custom_call_target="tpu_custom_call" | custom-call | flops 4294967296 | bytes 1572864 | tf_op jit(solution)/shard_map/pallas_call | solution.py:443
  43.0 1.5 %divide_convert_fusion = bf16[2048,128]{1,0:T(8,128)(2,1)} fusion(bf16[2048,128]{1,0:T(8,128)(2,1)S(1)} %get-tuple-element.7, f32[]{:T(128)} %bitcast.2), kind=kLoop, calls=%fused_computation | loop fusion | flops 786432 | bytes 1048580 | tf_op jit(solution)/shard_map/convert_element_type | solution.py:502

commit v3 on v2

--- a/solution.py
+++ b/solution.py
@@ -59,8 +59,7 @@
     bra_rows = select(entry == ((index >> 2 & 12) | (index & 3)))
     ket = dot(ket_rows, parts).astype(BF16)
     bra = dot(bra_rows, parts).astype(BF16)
-    ket_ref[:, : 2 * half] = ket
-    ket_ref[:, 2 * half :] = ket
+    ket_ref[...] = ket
     bra_ref[...] = bra
     total_ref[...] = jnp.zeros_like(total_ref)
 
@@ -76,11 +75,15 @@
         column = jnp.where(lanes < 2 * half, high, column - high)[:1]
         kets = jnp.where((entry & 60) == ket_place, column, 0.0).astype(BF16)
         bras = select((entry & 63) == bra_place + t)[:, : 2 * half]
-        total_ref[...] += dot_nt(kets, ket_ref[...]) * dot_nt(bras, bra_ref[...])
+        total_ref[...] += dot_nt(kets, jnp.concatenate([ket_ref[...]] * 2, axis=1)) * dot_nt(bras, bra_ref[...])
         return carry
 
     lax.fori_loop(0, S, add, 0)
     return total_ref[...].astype(BF16)
+
+
+def wide(ref):
+    return jnp.concatenate([ref[i] for i in range(ref.shape[0])], axis=1)
 
 
 def kernel(
@@ -115,6 +118,7 @@
     quad_ref,
     ring_ref,
     load_sem,
+    ready_sem,
     left_send,
     left_recv,
     relay_send,
@@ -148,10 +152,17 @@
         copy.start()
         return copy
 
-    load_factor = load(factor_hbm, factor_ref, 0)
-    load_front = load(front_hbm, front_ref, 1)
-    load_site = load(site_hbm, site_ref, 2)
-    load_operator = load(operator_hbm, operator_ref, 3)
+    def load_factor(i):
+        piece = pl.ds(pl.multiple_of(i * 2 * TILE, 2 * TILE), 2 * TILE)
+        return pltpu.make_async_copy(
+            factor_hbm.at[piece, :], factor_ref.at[piece, :], load_sem.at[3 + i]
+        )
+
+    for i in range(CHUNKS // 2):
+        load_factor(i).start()
+    load_site = load(site_hbm, site_ref, 1)
+    load_operator = load(operator_hbm, operator_ref, 2)
+    load_front = load(front_hbm, front_ref, 0)
 
     barrier = pltpu.get_barrier_semaphore()
 
@@ -162,7 +173,7 @@
         return place * QUAD + lax.rem(member + k, QUAD)
 
     def ring_column(k):
-        return lax.rem(place + k, n_ring) * QUAD + member
+        return lax.rem(place + k + n_ring, n_ring) * QUAD + member
 
     greet(row, before)
     greet(row, behind)
@@ -170,11 +181,23 @@
     for k in range(1, QUAD):
         greet(row, quad_column(k))
 
-    def greet_ring(k, carry):
+    def far_first(k):
+        return lax.rem(n_ring // 2 + n_ring + (2 * lax.rem(k, 2) - 1) * ((k + 1) // 2), n_ring)
+
+    for k in (1, 2):
         greet(partner, ring_column(k))
-        return carry
-
-    lax.fori_loop(1, n_ring, greet_ring, 0)
+        greet(partner, ring_column(-k))
+    greet(row, ring_column(2))
+    greet(row, ring_column(-2))
+
+    def tell(n):
+        for k in (-2 - 2 * n, 2 + 2 * n):
+            pl.semaphore_signal(
+                ready_sem.at[n],
+                inc=1,
+                device_id=(row, ring_column(k)),
+                device_id_type=MESH,
+            )
 
     relay = beside_x(row, column, 0)
     served = beside_x(row, column, 1)
@@ -199,26 +222,20 @@
         block = ref[rows_of(i, 2 * TILE), :]
         return jnp.concatenate([block[:TILE], block[TILE:]], axis=1)
 
-    swap_ref[...] = swap_16()
+    swap = swap_16()
+    swap_ref[0], swap_ref[1] = swap[:, :X], swap[:, X:]
     identity_ref[...] = select(iota((X, X), 0) == iota((X, X), 1))
-    load_factor.wait()
-    load_front.wait()
 
     def permute(i, carry):
+        load_factor(i).wait()
         kept = (iota((TILE, 2 * X), 1) & (X - 1)) < kept_ref[0, 0]
-        block = dot(swap_ref[...], beside(factor_ref, i))
+        block = dot(wide(swap_ref), beside(factor_ref, i))
         block = jnp.where(kept, block, 0.0).astype(BF16)
-        other = dot(swap_ref[...], beside(front_ref, i)).astype(BF16)
         for k in range(2):
             lanes = slice(k * X, (k + 1) * X)
             for q in range(D2):
                 start = pl.multiple_of(q * X + i * 2 * D2 + k * D2, D2)
                 planes_ref[pl.ds(start, D2), :] = block[q * D2 : (q + 1) * D2, lanes]
-            for v in range(D2):
-                start = pl.multiple_of(i * 2 * D2 + k * D2, D2)
-                front_planes_ref[pl.ds(start, D2), v * X : (v + 1) * X] = other[
-                    v * D2 : (v + 1) * D2, lanes
-                ]
         return carry
 
     lax.fori_loop(0, CHUNKS // 2, permute, 0)
@@ -239,14 +256,15 @@
 
     def interleave(i, carry):
         for n in range(2):
-            both = dot(swap_ref[...], beside(turned_ref, 2 * i + n)).astype(BF16)
+            both = dot(wide(swap_ref), beside(turned_ref, 2 * i + n)).astype(BF16)
             for k in range(2):
                 sent_ref[rows_of(4 * i + 2 * n + k, TILE), :] = both[:, k * X : (k + 1) * X]
         return carry
 
     lax.fori_loop(0, CHUNKS // 4, interleave, 0)
 
-    pl.semaphore_wait(barrier, 2 + 1 + (QUAD - 1) + (n_ring - 1) + 2 * core)
+    pl.semaphore_wait(barrier, 2 + 1 + (QUAD - 1) + 6 + 2 * core)
+    tell(0)
 
     def left_copy(i):
         return pltpu.make_async_remote_copy(
@@ -298,9 +316,22 @@
     def _():
         send_left(0)
 
+    def permute_front(i, carry):
+        both = dot(wide(swap_ref), beside(front_ref, i)).astype(BF16)
+        for k in range(2):
+            for v in range(D2):
+                start = pl.multiple_of(v * X + i * 2 * D2 + k * D2, D2)
+                front_planes_ref[pl.ds(start, D2), :] = both[
+                    v * D2 : (v + 1) * D2, k * X : (k + 1) * X
+                ]
+        return carry
+
+    load_front.wait()
+    lax.fori_loop(0, CHUNKS // 2, permute_front, 0)
     load_site.wait()
     load_operator.wait()
-    doubled_ref[...] = double_layer(site_ref[0], operator_ref, odd, ket_ref, bra_ref, total_ref)
+    doubled = double_layer(site_ref[0], operator_ref, odd, ket_ref, bra_ref, total_ref)
+    doubled_ref[0], doubled_ref[1] = doubled[:, :X], doubled[:, X:]
 
     @pl.when(core == 1)
     def _():
@@ -320,7 +351,11 @@
     def project(i):
         left = left_ref[rows_of(i, TILE), :]
         for v in range(0, D2, 2):
-            both = dot(left, front_planes_ref[:, v * X : (v + 2) * X]).astype(BF16)
+            pair = jnp.concatenate(
+                [front_planes_ref[v * X : (v + 1) * X], front_planes_ref[(v + 1) * X : (v + 2) * X]],
+                axis=1,
+            )
+            both = dot(left, pair).astype(BF16)
             for k in range(2):
                 projected_ref[:, (v + k) * D2 : (v + k + 1) * D2, :] = both[
                     :, k * X : (k + 1) * X
@@ -329,10 +364,10 @@
     def absorb():
         for a in range(0, D2, 2):
             pair = jnp.concatenate([projected_ref[a], projected_ref[a + 1]], axis=1)
-            both = dot(doubled_ref[...], pair).astype(BF16)
+            both = dot(wide(doubled_ref), pair).astype(BF16)
             for k in range(2):
                 for q in range(D2):
-                    absorbed_ref[(a + k) * D2 : (a + k + 1) * D2, q * X : (q + 1) * X] = both[
+                    absorbed_ref[q, (a + k) * D2 : (a + k + 1) * D2] = both[
                         q * D2 : (q + 1) * D2, k * X : (k + 1) * X
                     ]
 
@@ -349,9 +384,14 @@
         def _():
             pass_on(2 * i + 1)
 
+        @pl.when(i == 2)
+        def _():
+            pl.semaphore_wait(ready_sem.at[0], 2)
+            tell(1)
+
         absorb()
         project(jnp.minimum(i + 1, CHUNKS - 1))
-        result = dot(absorbed_ref[...], planes_ref[...])
+        result = dot(wide(absorbed_ref), planes_ref[...])
         unscaled_ref[rows_of(i, TILE), :] = result.astype(BF16)
         front_copy(i).start()
         return jnp.maximum(top, jnp.max(jnp.abs(result).reshape(TILE // 8, 8, X), axis=0))
@@ -381,13 +421,12 @@
             device_id_type=MESH,
         )
 
+    pl.semaphore_wait(ready_sem.at[1], 2)
     quad_ref[member] = top
     for k in range(1, QUAD):
         quad_copy(k).start()
     for k in range(1, QUAD):
         arrival(quad_ref, quad_recv, lax.rem(member + k, QUAD)).wait_recv()
-    for k in range(1, QUAD):
-        quad_copy(k).wait_send()
     ring_ref[n_ring] = jnp.max(quad_ref[...], axis=0)
 
     def ring_copy(k):
@@ -401,7 +440,7 @@
         )
 
     def start_ring(k, carry):
-        ring_copy(k).start()
+        ring_copy(far_first(k)).start()
         return carry
 
     def end_ring(k, carry):
@@ -412,7 +451,10 @@
     lax.fori_loop(0, n_ring, start_ring, 0)
     lax.fori_loop(0, n_ring, end_ring, 0)
     largest = jnp.max(ring_ref[:n_ring], axis=0)
-    divisor_ref[...] = jnp.max(largest, axis=1, keepdims=True) + EPSILON
+    divisor_ref[0, 0] = jnp.max(largest) + EPSILON
+
+    for k in range(1, QUAD):
+        quad_copy(k).wait_send()
 
     def finish(i, carry):
         left_copy(i).wait_send()
@@ -432,7 +474,6 @@
     rows = X * D2
     smem = pl.BlockSpec(memory_space=pltpu.SMEM)
     hbm = pl.BlockSpec(memory_space=pltpu.HBM)
-    vmem = pl.BlockSpec(memory_space=pltpu.VMEM)
     anywhere = pl.BlockSpec(memory_space=pl.ANY)
     dma = pltpu.SemaphoreType.DMA
 
@@ -447,7 +488,7 @@
             jax.ShapeDtypeStruct((1, 1), F32),
         ),
         in_specs=[smem] + [hbm] * 4,
-        out_specs=(anywhere, vmem),
+        out_specs=(anywhere, smem),
         scratch_shapes=[
             pltpu.SMEM(operators.shape, F32),
             pltpu.VMEM(site_tensors.shape, F32),
@@ -458,19 +499,20 @@
             pltpu.VMEM((rows, X), BF16),
             pltpu.VMEM((rows, X), BF16),
             pltpu.VMEM((rows // 2, X), BF16),
-            pltpu.VMEM((X, rows), BF16),
-            pltpu.VMEM((TILE, TILE), BF16),
+            pltpu.VMEM((rows, X), BF16),
+            pltpu.VMEM((2, TILE, X), BF16),
             pltpu.VMEM((X, X), BF16),
-            pltpu.VMEM((TILE, TILE), BF16),
+            pltpu.VMEM((TILE, X), BF16),
             pltpu.VMEM((TILE, X), BF16),
             pltpu.VMEM((TILE, TILE), F32),
-            pltpu.VMEM((TILE, TILE), BF16),
+            pltpu.VMEM((2, TILE, X), BF16),
             pltpu.VMEM((D2, TILE, X), BF16),
-            pltpu.VMEM((TILE, rows), BF16),
+            pltpu.VMEM((D2, TILE, X), BF16),
             pltpu.VMEM((rows, X), BF16),
             pltpu.VMEM((QUAD, 1, X), F32),
             pltpu.VMEM((n_columns // QUAD + 1, 1, X), F32),
-            dma((4,)),
+            dma((3 + CHUNKS // 2,)),
+            pltpu.SemaphoreType.REGULAR((2,)),
             dma((CHUNKS,)),
             dma((CHUNKS,)),
             dma((CHUNKS // 2,)),

time: 44.6 us -> 44.3 us (level)
  no operation moved by 1% of the time
where the time goes in v3:
time: 44.3 us; the launch traced here: 44.2 us
  Pallas kernels  42.1 us (95%)
  other arithmetic  1.46 us (3%)
  between operations  0.66 us (1%)
    pallas_call x1, Pallas kernels, per_device(): pl.pallas_call(body, out_shape=(jax.ShapeDtypeStruct((rows, X), BF16), ja...  42.1 us
    convert_element_type x1, other arithmetic, per_device(): return normalized.astype(BF16).reshape(1, X, D2, X)  1.46 us

profile of v3, /device:TPU:1, one launch (start us, length us, event | category | flops | bytes accessed | tf_op | source)
XLA Modules:
  0.0 44.2 jit_solution(4335644304985246476)
XLA Ops:
  0.7 42.1 %shard_map.55 = (bf16[2048,128]{1,0:T(8,128)(2,1)S(1)}, f32[1,1]{1,0:T(1,128)}) custom-call(s32[1,1]{1,0:T(1,128)S(6)} %copy.6.refs_0_, f32[1,4,4]{2,1,0:T(4,128)} %refs_1_.1, f32[1,16,64]{2,1,0:T(8,128)} %refs_2_.1, bf16[2048,128]{1,0:T(8,128)(2,1)} %bitcast.4, bf16[2048,128]{1,0:T(8,128)(2,1)} %bitcast.5), custom_call_target="tpu_custom_call" | custom-call | flops 4294967296 | bytes 1572864 | tf_op jit(solution)/shard_map/pallas_call | solution.py:484
  42.7 1.5 %divide_convert_fusion = bf16[2048,128]{1,0:T(8,128)(2,1)} fusion(bf16[2048,128]{1,0:T(8,128)(2,1)S(1)} %get-tuple-element.7, f32[]{:T(128)} %bitcast.2), kind=kLoop, calls=%fused_computation | loop fusion | flops 786432 | bytes 1048580 | tf_op jit(solution)/shard_map/convert_element_type | solution.py:544

commit v4 on v3

--- a/solution.py
+++ b/solution.py
@@ -241,27 +241,23 @@
     lax.fori_loop(0, CHUNKS // 2, permute, 0)
 
     def turn(i, carry):
-        for n in range(2):
-            block = planes_ref[rows_of(2 * i + n, 2 * X), :]
+        for n in range(4):
+            block = planes_ref[rows_of(4 * i + n, 2 * X), :]
             both = dot_nt(identity_ref[...], block).astype(BF16)
             for k in range(2):
                 for j in range(CHUNKS):
-                    start = pl.multiple_of(j * TILE + (4 * i + 2 * n + k) * D2, D2)
+                    start = pl.multiple_of(j * TILE + (8 * i + 2 * n + k) * D2, D2)
                     turned_ref[pl.ds(start, D2), :] = both[
                         j * D2 : (j + 1) * D2, k * X : (k + 1) * X
                     ]
         return carry
 
-    lax.fori_loop(0, D2 // 4, turn, 0)
-
-    def interleave(i, carry):
-        for n in range(2):
-            both = dot(wide(swap_ref), beside(turned_ref, 2 * i + n)).astype(BF16)
-            for k in range(2):
-                sent_ref[rows_of(4 * i + 2 * n + k, TILE), :] = both[:, k * X : (k + 1) * X]
-        return carry
-
-    lax.fori_loop(0, CHUNKS // 4, interleave, 0)
+    lax.fori_loop(0, D2 // 8, turn, 0)
+
+    for i in range(CHUNKS // 2):
+        both = dot(wide(swap_ref), beside(turned_ref, i)).astype(BF16)
+        for k in range(2):
+            sent_ref[rows_of(2 * i + k, TILE), :] = both[:, k * X : (k + 1) * X]
 
     pl.semaphore_wait(barrier, 2 + 1 + (QUAD - 1) + 6 + 2 * core)
     tell(0)
@@ -279,26 +275,22 @@
     def relay_copy(i):
         return pltpu.make_async_remote_copy(
             src_ref=chunk(sent_ref, i),
-            dst_ref=chunk(relay_ref, i // 2),
+            dst_ref=chunk(relay_ref, i // 2 - 1),
             send_sem=left_send.at[i],
-            recv_sem=relay_recv.at[i // 2],
+            recv_sem=relay_recv.at[i // 2 - 1],
             device_id=relay,
             device_id_type=MESH,
         )
 
     def onward_copy(i):
         return pltpu.make_async_remote_copy(
-            src_ref=chunk(relay_ref, i // 2),
+            src_ref=chunk(relay_ref, i // 2 - 1),
             dst_ref=chunk(left_ref, i),
-            send_sem=relay_send.at[i // 2],
+            send_sem=relay_send.at[i // 2 - 1],
             recv_sem=left_recv.at[i],
             device_id=served_target,
             device_id_type=MESH,
         )
-
-    def send_left(i):
-        left_copy(i).start()
-        relay_copy(i + 1).start()
 
     def pass_on(i):
         relay_copy(i).wait_recv()
@@ -314,29 +306,32 @@
 
     @pl.when(core == 1)
     def _():
-        send_left(0)
+        left_copy(0).start()
+        relay_copy(2).start()
 
     def permute_front(i, carry):
-        both = dot(wide(swap_ref), beside(front_ref, i)).astype(BF16)
-        for k in range(2):
-            for v in range(D2):
-                start = pl.multiple_of(v * X + i * 2 * D2 + k * D2, D2)
-                front_planes_ref[pl.ds(start, D2), :] = both[
-                    v * D2 : (v + 1) * D2, k * X : (k + 1) * X
-                ]
+        for n in range(2):
+            both = dot(wide(swap_ref), beside(front_ref, 2 * i + n)).astype(BF16)
+            for k in range(2):
+                for v in range(D2):
+                    start = pl.multiple_of(v * X + (4 * i + 2 * n + k) * D2, D2)
+                    front_planes_ref[pl.ds(start, D2), :] = both[
+                        v * D2 : (v + 1) * D2, k * X : (k + 1) * X
+                    ]
         return carry
 
     load_front.wait()
-    lax.fori_loop(0, CHUNKS // 2, permute_front, 0)
+    lax.fori_loop(0, CHUNKS // 4, permute_front, 0)
+
+    @pl.when(core == 1)
+    def _():
+        left_copy(1).start()
+        relay_copy(4).start()
+
     load_site.wait()
     load_operator.wait()
     doubled = double_layer(site_ref[0], operator_ref, odd, ket_ref, bra_ref, total_ref)
     doubled_ref[0], doubled_ref[1] = doubled[:, :X], doubled[:, X:]
-
-    @pl.when(core == 1)
-    def _():
-        send_left(2)
-        pass_on(1)
 
     def front_copy(i):
         return pltpu.make_async_remote_copy(
@@ -376,13 +371,14 @@
         def _():
             left_copy(i + 1).wait_recv()
 
-        @pl.when((core == 1) & (i < CHUNKS // 2 - 2))
+        @pl.when((core == 1) & (i < CHUNKS // 2 - 1))
         def _():
-            send_left(2 * i + 4)
-
-        @pl.when((core == 1) & (i >= 1) & (i < CHUNKS // 2))
+            pass_on(2 * i + 2)
+            left_copy(2 * i + 3).start()
+
+        @pl.when((core == 1) & (i == 0))
         def _():
-            pass_on(2 * i + 1)
+            relay_copy(6).start()
 
         @pl.when(i == 2)
         def _():
@@ -465,7 +461,7 @@
 
     @pl.when(core == 1)
     def _():
-        for i in range(1, CHUNKS, 2):
+        for i in range(2, CHUNKS, 2):
             onward_copy(i).wait_send()
 
 

time: 44.3 us -> 42.5 us (0.959)
  Pallas kernels: 42.1 us -> 40.2 us
    pallas_call x1, Pallas kernels: 42.1 us -> 40.2 us  [per_device(): pl.pallas_call(body, out_shape=(jax.ShapeDtypeStruct((rows, X), BF16), ja...]
where the time goes in v4:
time: 42.5 us; the launch traced here: 42.3 us
  Pallas kernels  40.2 us (95%)
  other arithmetic  1.46 us (3%)
  between operations  0.66 us (2%)
    pallas_call x1, Pallas kernels, per_device(): pl.pallas_call(body, out_shape=(jax.ShapeDtypeStruct((rows, X), BF16), ja...  40.2 us
    convert_element_type x1, other arithmetic, per_device(): return normalized.astype(BF16).reshape(1, X, D2, X)  1.46 us

profile of v4, /device:TPU:1, one launch (start us, length us, event | category | flops | bytes accessed | tf_op | source)
XLA Modules:
  0.0 42.3 jit_solution(1818561873227023713)
XLA Ops:
  0.7 40.2 %shard_map.55 = (bf16[2048,128]{1,0:T(8,128)(2,1)S(1)}, f32[1,1]{1,0:T(1,128)}) custom-call(s32[1,1]{1,0:T(1,128)S(6)} %copy.6.refs_0_, f32[1,4,4]{2,1,0:T(4,128)} %refs_1_.1, f32[1,16,64]{2,1,0:T(8,128)} %refs_2_.1, bf16[2048,128]{1,0:T(8,128)(2,1)} %bitcast.4, bf16[2048,128]{1,0:T(8,128)(2,1)} %bitcast.5), custom_call_target="tpu_custom_call" | custom-call | flops 4294967296 | bytes 1572864 | tf_op jit(solution)/shard_map/pallas_call | solution.py:480
  40.9 1.5 %divide_convert_fusion = bf16[2048,128]{1,0:T(8,128)(2,1)} fusion(bf16[2048,128]{1,0:T(8,128)(2,1)S(1)} %get-tuple-element.7, f32[]{:T(128)} %bitcast.2), kind=kLoop, calls=%fused_computation | loop fusion | flops 786432 | bytes 1048580 | tf_op jit(solution)/shard_map/convert_element_type | solution.py:540

commit v5 on v4

--- a/solution.py
+++ b/solution.py
@@ -275,18 +275,18 @@
     def relay_copy(i):
         return pltpu.make_async_remote_copy(
             src_ref=chunk(sent_ref, i),
-            dst_ref=chunk(relay_ref, i // 2 - 1),
+            dst_ref=chunk(relay_ref, (i - 3) // 2),
             send_sem=left_send.at[i],
-            recv_sem=relay_recv.at[i // 2 - 1],
+            recv_sem=relay_recv.at[(i - 3) // 2],
             device_id=relay,
             device_id_type=MESH,
         )
 
     def onward_copy(i):
         return pltpu.make_async_remote_copy(
-            src_ref=chunk(relay_ref, i // 2 - 1),
+            src_ref=chunk(relay_ref, (i - 3) // 2),
             dst_ref=chunk(left_ref, i),
-            send_sem=relay_send.at[i // 2 - 1],
+            send_sem=relay_send.at[(i - 3) // 2],
             recv_sem=left_recv.at[i],
             device_id=served_target,
             device_id_type=MESH,
@@ -307,7 +307,7 @@
     @pl.when(core == 1)
     def _():
         left_copy(0).start()
-        relay_copy(2).start()
+        relay_copy(3).start()
 
     def permute_front(i, carry):
         for n in range(2):
@@ -326,12 +326,16 @@
     @pl.when(core == 1)
     def _():
         left_copy(1).start()
-        relay_copy(4).start()
+        relay_copy(5).start()
 
     load_site.wait()
     load_operator.wait()
     doubled = double_layer(site_ref[0], operator_ref, odd, ket_ref, bra_ref, total_ref)
     doubled_ref[0], doubled_ref[1] = doubled[:, :X], doubled[:, X:]
+
+    @pl.when(core == 1)
+    def _():
+        left_copy(2).start()
 
     def front_copy(i):
         return pltpu.make_async_remote_copy(
@@ -345,24 +349,21 @@
 
     def project(i):
         left = left_ref[rows_of(i, TILE), :]
-        for v in range(0, D2, 2):
-            pair = jnp.concatenate(
-                [front_planes_ref[v * X : (v + 1) * X], front_planes_ref[(v + 1) * X : (v + 2) * X]],
-                axis=1,
-            )
-            both = dot(left, pair).astype(BF16)
-            for k in range(2):
-                projected_ref[:, (v + k) * D2 : (v + k + 1) * D2, :] = both[
+        for v in range(0, D2, 4):
+            four = [front_planes_ref[(v + k) * X : (v + k + 1) * X] for k in range(4)]
+            result = dot(left, jnp.concatenate(four, axis=1)).astype(BF16)
+            for k in range(4):
+                projected_ref[:, (v + k) * D2 : (v + k + 1) * D2, :] = result[
                     :, k * X : (k + 1) * X
                 ].reshape(D2, D2, X)
 
     def absorb():
-        for a in range(0, D2, 2):
-            pair = jnp.concatenate([projected_ref[a], projected_ref[a + 1]], axis=1)
-            both = dot(wide(doubled_ref), pair).astype(BF16)
-            for k in range(2):
+        for a in range(0, D2, 4):
+            four = [projected_ref[a + k] for k in range(4)]
+            result = dot(wide(doubled_ref), jnp.concatenate(four, axis=1)).astype(BF16)
+            for k in range(4):
                 for q in range(D2):
-                    absorbed_ref[q, (a + k) * D2 : (a + k + 1) * D2] = both[
+                    absorbed_ref[q, (a + k) * D2 : (a + k + 1) * D2] = result[
                         q * D2 : (q + 1) * D2, k * X : (k + 1) * X
                     ]
 
@@ -371,14 +372,18 @@
         def _():
             left_copy(i + 1).wait_recv()
 
-        @pl.when((core == 1) & (i < CHUNKS // 2 - 1))
+        @pl.when((core == 1) & (i < 2))
         def _():
-            pass_on(2 * i + 2)
-            left_copy(2 * i + 3).start()
+            pass_on(2 * i + 3)
+            left_copy(2 * i + 4).start()
 
         @pl.when((core == 1) & (i == 0))
         def _():
-            relay_copy(6).start()
+            relay_copy(7).start()
+
+        @pl.when((core == 1) & (i == 3))
+        def _():
+            pass_on(7)
 
         @pl.when(i == 2)
         def _():
@@ -461,7 +466,7 @@
 
     @pl.when(core == 1)
     def _():
-        for i in range(2, CHUNKS, 2):
+        for i in range(3, CHUNKS, 2):
             onward_copy(i).wait_send()
 
 

time: 42.5 us -> 42.8 us (level)
  the two profiles are of different devices: /device:TPU:1 before, /device:TPU:20 now
where the time goes in v5:
time: 42.8 us; the launch traced here: 42.7 us
  Pallas kernels  40.5 us (95%)
  other arithmetic  1.46 us (3%)
  between operations  0.66 us (2%)
    pallas_call x1, Pallas kernels, per_device(): pl.pallas_call(body, out_shape=(jax.ShapeDtypeStruct((rows, X), BF16), ja...  40.5 us
    convert_element_type x1, other arithmetic, per_device(): return normalized.astype(BF16).reshape(1, X, D2, X)  1.46 us

profile of v5, /device:TPU:20, one launch (start us, length us, event | category | flops | bytes accessed | tf_op | source)
XLA Modules:
  0.0 42.7 jit_solution(9433829553562484337)
XLA Ops:
  0.7 40.5 %shard_map.55 = (bf16[2048,128]{1,0:T(8,128)(2,1)S(1)}, f32[1,1]{1,0:T(1,128)}) custom-call(s32[1,1]{1,0:T(1,128)S(6)} %copy.6.refs_0_, f32[1,4,4]{2,1,0:T(4,128)} %refs_1_.1, f32[1,16,64]{2,1,0:T(8,128)} %refs_2_.1, bf16[2048,128]{1,0:T(8,128)(2,1)} %bitcast.4, bf16[2048,128]{1,0:T(8,128)(2,1)} %bitcast.5), custom_call_target="tpu_custom_call" | custom-call | flops 4294967296 | bytes 1572864 | tf_op jit(solution)/shard_map/pallas_call | solution.py:485
  41.2 1.5 %divide_convert_fusion = bf16[2048,128]{1,0:T(8,128)(2,1)} fusion(bf16[2048,128]{1,0:T(8,128)(2,1)S(1)} %get-tuple-element.7, f32[]{:T(128)} %bitcast.2), kind=kLoop, calls=%fused_computation | loop fusion | flops 786432 | bytes 1048580 | tf_op jit(solution)/shard_map/convert_element_type | solution.py:545

commit v6 on v5

--- a/solution.py
+++ b/solution.py
@@ -254,11 +254,12 @@
 
     lax.fori_loop(0, D2 // 8, turn, 0)
 
-    for i in range(CHUNKS // 2):
+    def interleave(i):
         both = dot(wide(swap_ref), beside(turned_ref, i)).astype(BF16)
         for k in range(2):
             sent_ref[rows_of(2 * i + k, TILE), :] = both[:, k * X : (k + 1) * X]
 
+    interleave(0)
     pl.semaphore_wait(barrier, 2 + 1 + (QUAD - 1) + 6 + 2 * core)
     tell(0)
 
@@ -300,13 +301,16 @@
         left_copy(i).start()
         return carry
 
+    left_copy(0).start()
+    for i in range(1, CHUNKS // 2):
+        interleave(i)
+
     @pl.when(core == 0)
     def _():
-        lax.fori_loop(0, CHUNKS, start_left, 0)
+        lax.fori_loop(1, CHUNKS, start_left, 0)
 
     @pl.when(core == 1)
     def _():
-        left_copy(0).start()
         relay_copy(3).start()
 
     def permute_front(i, carry):

time: 42.8 us -> 42.2 us (0.986)
  the two profiles are of different devices: /device:TPU:20 before, /device:TPU:1 now
where the time goes in v6:
time: 42.2 us; the launch traced here: 42.1 us
  Pallas kernels  39.9 us (95%)
  other arithmetic  1.46 us (3%)
  between operations  0.66 us (2%)
    pallas_call x1, Pallas kernels, per_device(): pl.pallas_call(body, out_shape=(jax.ShapeDtypeStruct((rows, X), BF16), ja...  39.9 us
    convert_element_type x1, other arithmetic, per_device(): return normalized.astype(BF16).reshape(1, X, D2, X)  1.46 us

profile of v6, /device:TPU:1, one launch (start us, length us, event | category | flops | bytes accessed | tf_op | source)
XLA Modules:
  0.0 42.1 jit_solution(5806079802049987232)
XLA Ops:
  0.7 39.9 %shard_map.55 = (bf16[2048,128]{1,0:T(8,128)(2,1)S(1)}, f32[1,1]{1,0:T(1,128)}) custom-call(s32[1,1]{1,0:T(1,128)S(6)} %copy.6.refs_0_, f32[1,4,4]{2,1,0:T(4,128)} %refs_1_.1, f32[1,16,64]{2,1,0:T(8,128)} %refs_2_.1, bf16[2048,128]{1,0:T(8,128)(2,1)} %bitcast.4, bf16[2048,128]{1,0:T(8,128)(2,1)} %bitcast.5), custom_call_target="tpu_custom_call" | custom-call | flops 4294967296 | bytes 1572864 | tf_op jit(solution)/shard_map/pallas_call | solution.py:489
  40.6 1.5 %divide_convert_fusion = bf16[2048,128]{1,0:T(8,128)(2,1)} fusion(bf16[2048,128]{1,0:T(8,128)(2,1)S(1)} %get-tuple-element.7, f32[]{:T(128)} %bitcast.2), kind=kLoop, calls=%fused_computation | loop fusion | flops 786432 | bytes 1048580 | tf_op jit(solution)/shard_map/convert_element_type | solution.py:549

commit v7 on v6

--- a/solution.py
+++ b/solution.py
@@ -353,21 +353,24 @@
 
     def project(i):
         left = left_ref[rows_of(i, TILE), :]
-        for v in range(0, D2, 4):
-            four = [front_planes_ref[(v + k) * X : (v + k + 1) * X] for k in range(4)]
-            result = dot(left, jnp.concatenate(four, axis=1)).astype(BF16)
-            for k in range(4):
-                projected_ref[:, (v + k) * D2 : (v + k + 1) * D2, :] = result[
+        for v in range(0, D2, 2):
+            pair = jnp.concatenate(
+                [front_planes_ref[v * X : (v + 1) * X], front_planes_ref[(v + 1) * X : (v + 2) * X]],
+                axis=1,
+            )
+            both = dot(left, pair).astype(BF16)
+            for k in range(2):
+                projected_ref[:, (v + k) * D2 : (v + k + 1) * D2, :] = both[
                     :, k * X : (k + 1) * X
                 ].reshape(D2, D2, X)
 
     def absorb():
-        for a in range(0, D2, 4):
-            four = [projected_ref[a + k] for k in range(4)]
-            result = dot(wide(doubled_ref), jnp.concatenate(four, axis=1)).astype(BF16)
-            for k in range(4):
+        for a in range(0, D2, 2):
+            pair = jnp.concatenate([projected_ref[a], projected_ref[a + 1]], axis=1)
+            both = dot(wide(doubled_ref), pair).astype(BF16)
+            for k in range(2):
                 for q in range(D2):
-                    absorbed_ref[q, (a + k) * D2 : (a + k + 1) * D2] = result[
+                    absorbed_ref[q, (a + k) * D2 : (a + k + 1) * D2] = both[
                         q * D2 : (q + 1) * D2, k * X : (k + 1) * X
                     ]
 

time: 42.2 us -> 42.2 us (level)
  no operation moved by 1% of the time
where the time goes in v7:
time: 42.2 us; the launch traced here: 42.1 us
  Pallas kernels  39.9 us (95%)
  other arithmetic  1.46 us (3%)
  between operations  0.66 us (2%)
    pallas_call x1, Pallas kernels, per_device(): pl.pallas_call(body, out_shape=(jax.ShapeDtypeStruct((rows, X), BF16), ja...  39.9 us
    convert_element_type x1, other arithmetic, per_device(): return normalized.astype(BF16).reshape(1, X, D2, X)  1.46 us

profile of v7, /device:TPU:1, one launch (start us, length us, event | category | flops | bytes accessed | tf_op | source)
XLA Modules:
  0.0 42.1 jit_solution(15950137599594100626)
XLA Ops:
  0.7 39.9 %shard_map.55 = (bf16[2048,128]{1,0:T(8,128)(2,1)S(1)}, f32[1,1]{1,0:T(1,128)}) custom-call(s32[1,1]{1,0:T(1,128)S(6)} %copy.6.refs_0_, f32[1,4,4]{2,1,0:T(4,128)} %refs_1_.1, f32[1,16,64]{2,1,0:T(8,128)} %refs_2_.1, bf16[2048,128]{1,0:T(8,128)(2,1)} %bitcast.4, bf16[2048,128]{1,0:T(8,128)(2,1)} %bitcast.5), custom_call_target="tpu_custom_call" | custom-call | flops 4294967296 | bytes 1572864 | tf_op jit(solution)/shard_map/pallas_call | solution.py:492
  40.6 1.5 %divide_convert_fusion = bf16[2048,128]{1,0:T(8,128)(2,1)} fusion(bf16[2048,128]{1,0:T(8,128)(2,1)S(1)} %get-tuple-element.7, f32[]{:T(128)} %bitcast.2), kind=kLoop, calls=%fused_computation | loop fusion | flops 786432 | bytes 1048580 | tf_op jit(solution)/shard_map/convert_element_type | solution.py:552
